TPU v7x, 32 devices: a whole 2x2x4 slice. The times are simulated.
32 devices in a mesh: dp: 16 (over z, x, core), tensor: 2 (over y).
Axes of the slice: x: 2, y: 2, z: 4, core: 2. Of those that a mesh axis runs over, the one named last changes fastest.
Arguments:
- tokens: bfloat16 [6304, 768], P(('dp', 'tensor')), may hold values from -6 to 6
- w_qkv: bfloat16 [768, 3, 768], P('dp', None, 'tensor'), may hold values from -0.21875 to 0.21875
- w_mix: bfloat16 [768, 768], P('dp', 'tensor'), may hold values from -0.875 to 0.875
- w_router: bfloat16 [768, 16], P('dp'), may hold values from -0.15625 to 0.15625
- gain_one: bfloat16 [768], P('dp'), may hold values from 0.5 to 1.5
- shift_one: bfloat16 [768], P('dp'), may hold values from -1 to 1
- gain_two: bfloat16 [768], P('dp'), may hold values from 0.5 to 1.5
- shift_two: bfloat16 [768], P('dp'), may hold values from -1 to 1
- w_expand: bfloat16 [16, 768, 3072], P('dp', None, 'tensor'), may hold values from -0.21875 to 0.21875
- w_shrink: bfloat16 [16, 3072, 768], P('dp', 'tensor'), may hold values from -0.109375 to 0.109375
- expert_ids: int32 [6304, 2], P('dp'), may hold values from 0 to 15, as said below
- slot_ids: int32 [6304, 2], P('dp'), may hold values from 0 to 63, as said below
- keep_mask: int32 [6304, 2], P('dp'), may hold values from 0 to 1
- out_grad: bfloat16 [6304, 768], P(('dp', 'tensor')), may hold values from -6 to 6
Outputs:
- block_out: bfloat16 [6304, 768], P(('dp', 'tensor'))
- grad_tokens: float32 [6304, 768], P(('dp', 'tensor'))
- grad_w_qkv: float32 [768, 3, 768], P('dp', None, 'tensor')
- grad_w_mix: float32 [768, 768], P('dp', 'tensor')
- grad_router: float32 [768, 16], P(('dp', 'tensor'))
- grad_gain_one: float32 [768], P(('dp', 'tensor'))
- grad_shift_one: float32 [768], P(('dp', 'tensor'))
- grad_gain_two: float32 [768], P(('dp', 'tensor'))
- grad_shift_two: float32 [768], P(('dp', 'tensor'))
- grad_w_expand: float32 [16, 768, 3072], P('dp', None, 'tensor')
- grad_w_shrink: float32 [16, 3072, 768], P('dp', 'tensor')
Inputs may be any that keep to these rules, and one draw needn't show every extreme that they name: `expert_ids`: the two experts of a token differ. `slot_ids`: among the kept routes of the 394 rows of one index of dp, no two share an expert and a slot; a dropped route has slot 0.
All inputs are finite; a program needn't handle non-finite values.
Results may differ from a plain program's by a relative error of at most 0.017.
Values may be sent and summed in bfloat16 or wider, within the bound.
A program may use at most 128 MiB of HBM per device.

v0:
```python
import jax
import jax.numpy as jnp
from jax import lax
from jax.sharding import PartitionSpec as P

DH = 64
SEQ = 197


def norm_rows(values, gain, shift):
    centre = values - jnp.mean(values, axis=-1, keepdims=True)
    spread = jnp.mean(centre * centre, axis=-1, keepdims=True)
    return centre * lax.rsqrt(spread + 1e-06) * gain + shift


def fetch(shards):
    return (
        lax.all_gather(shards[0], "dp", axis=0, tiled=True),
        lax.all_gather(shards[1], "dp", axis=0, tiled=True),
        lax.all_gather(shards[2], "dp", axis=0, tiled=True),
        lax.all_gather(shards[3], "dp", axis=0, tiled=True),
        lax.all_gather(shards[4], "dp", axis=0, tiled=True),
        lax.all_gather(shards[5], "dp", axis=0, tiled=True),
        lax.all_gather(shards[6], "dp", axis=0, tiled=True),
    )


def share_rows(values):
    return lax.all_gather(values, "tensor", axis=0, tiled=True)


def reduce_rows(values):
    return lax.psum_scatter(
        values.astype(jnp.bfloat16), "tensor", scatter_dimension=0, tiled=True
    ).astype(jnp.float32)


def send_out(buffer):
    return lax.all_to_all(buffer, "dp", split_axis=0, concat_axis=0, tiled=True)


def pick_routes(buffer, dest):
    width = buffer.shape[-1]
    flat = jnp.concatenate([buffer.reshape(-1, width), jnp.zeros((1, width), buffer.dtype)], 0)
    return (
        jnp.take(flat, dest.reshape(-1), axis=0)
        .reshape(dest.shape[0], 2, width)
        .astype(jnp.float32)
    )


def bring_back(values, expert_ids, slot_ids, keep_mask):
    experts, slots, width = values.shape
    arrived = lax.all_to_all(values, "dp", split_axis=0, concat_axis=0, tiled=True)
    dest = jnp.where(keep_mask > 0, expert_ids * slots + slot_ids, experts * slots)
    return pick_routes(arrived, dest)


def split_heads(mixed, images, head_size):
    heads = mixed.shape[2] // head_size
    shaped = mixed.reshape(images, -1, 3, heads, head_size)
    return (shaped[:, :, 0], shaped[:, :, 1], shaped[:, :, 2])


def attend(mixed, images, head_size):
    query, key_rows, value_rows = split_heads(mixed, images, head_size)
    scores = jnp.einsum(
        "ishd,ithd->ihst", query, key_rows, preferred_element_type=jnp.float32
    ) * head_size ** (-0.5)
    highest_score = jnp.max(scores, axis=-1, keepdims=True)
    total = jnp.sum(jnp.exp(scores - highest_score), axis=-1, keepdims=True)
    log_total = highest_score + jnp.log(total)
    weights = jnp.exp(scores - log_total).astype(jnp.bfloat16)
    heads_out = jnp.einsum(
        "ihst,ithd->ishd", weights, value_rows, preferred_element_type=jnp.float32
    )
    return (heads_out.reshape(mixed.shape[0], -1).astype(jnp.bfloat16), log_total)


def attend_back(mixed, log_total, grad_heads, images, head_size):
    query, key_rows, value_rows = split_heads(mixed, images, head_size)
    scale = head_size ** (-0.5)
    scores = (
        jnp.einsum("ishd,ithd->ihst", query, key_rows, preferred_element_type=jnp.float32) * scale
    )
    probs = jnp.exp(scores - log_total)
    weights = probs.astype(jnp.bfloat16)
    grad_shaped = grad_heads.reshape(query.shape)
    grad_weights = jnp.einsum(
        "ishd,ithd->ihst", grad_shaped, value_rows, preferred_element_type=jnp.float32
    )
    grad_values = jnp.einsum(
        "ihst,ishd->ithd", weights, grad_shaped, preferred_element_type=jnp.float32
    )
    grad_scores = (
        probs * (grad_weights - jnp.sum(probs * grad_weights, axis=-1, keepdims=True))
    ).astype(jnp.bfloat16)
    grad_query = (
        jnp.einsum("ihst,ithd->ishd", grad_scores, key_rows, preferred_element_type=jnp.float32)
        * scale
    )
    grad_keys = (
        jnp.einsum("ihst,ishd->ithd", grad_scores, query, preferred_element_type=jnp.float32)
        * scale
    )
    stacked = jnp.stack([grad_query, grad_keys, grad_values], axis=2)
    return stacked.reshape(mixed.shape[0], 3, -1)


def body(
    tokens,
    w_qkv,
    w_mix,
    w_router,
    gain_one,
    shift_one,
    gain_two,
    shift_two,
    w_expand,
    w_shrink,
    expert_ids,
    slot_ids,
    keep_mask,
    out_grad,
):
    highest = lax.Precision.HIGHEST
    contract_rows = (((0,), (0,)), ((), ()))
    contract_cols = (((1,), (1,)), ((), ()))
    width = tokens.shape[1]
    group = expert_ids.shape[0]
    images = group // SEQ
    experts = lax.axis_size("dp")
    slots = 2 * max(1, 2 * group * 2 // 3 // experts)
    shards = (w_qkv, w_mix, w_router, gain_one, shift_one, gain_two, shift_two)
    qkv_full, mix_full, router_full, gain_a, shift_a, gain_b, shift_b = fetch(shards)
    gain_a = gain_a.astype(jnp.float32)
    shift_a = shift_a.astype(jnp.float32)
    gain_b = gain_b.astype(jnp.float32)
    shift_b = shift_b.astype(jnp.float32)
    resid = tokens.astype(jnp.float32)
    group_a = share_rows(norm_rows(resid, gain_a, shift_a).astype(jnp.bfloat16))
    mixed = jnp.einsum("rd,dcf->rcf", group_a, qkv_full, preferred_element_type=jnp.float32).astype(
        jnp.bfloat16
    )
    heads_out, log_total = attend(mixed, images, DH)
    branch_a = lax.psum_scatter(
        lax.dot_general(
            heads_out, mix_full, contract_cols, preferred_element_type=jnp.float32
        ).astype(jnp.bfloat16),
        "tensor",
        scatter_dimension=0,
        tiled=True,
    ).astype(jnp.float32)
    resid_b = resid + branch_a
    group_b = share_rows(norm_rows(resid_b, gain_b, shift_b).astype(jnp.bfloat16))
    logits = jnp.dot(group_b, router_full, preferred_element_type=jnp.float32)
    onehot = expert_ids[:, :, None] == jnp.arange(experts, dtype=jnp.int32)[None, None, :]
    chosen = jnp.sum(jnp.where(onehot, logits[:, None, :], 0.0), axis=-1)
    pick = jax.nn.softmax(chosen, axis=-1)
    keep_float = keep_mask.astype(jnp.float32)
    gates = pick * keep_float
    dest = jnp.where(keep_mask > 0, expert_ids * slots + slot_ids, experts * slots)
    route_index = jnp.arange(2 * group, dtype=jnp.int32).reshape(group, 2)
    table = jnp.full((experts * slots + 1,), 2 * group, jnp.int32)
    table = table.at[dest.reshape(-1)].set(route_index.reshape(-1))[:-1]
    padded_rows = jnp.concatenate([group_b, jnp.zeros((1, width), jnp.bfloat16)], 0)
    sent = jnp.take(padded_rows, table // 2, axis=0).reshape(experts, slots, width)
    arrived = send_out(sent).reshape(-1, width)
    expand_here = w_expand[0]
    shrink_here = w_shrink[0]
    inner = jnp.dot(arrived, expand_here, preferred_element_type=jnp.float32)
    active = jax.nn.gelu(inner).astype(jnp.bfloat16)
    result = jnp.dot(active, shrink_here, preferred_element_type=jnp.float32).astype(jnp.bfloat16)
    route_out = bring_back(result.reshape(experts, slots, width), expert_ids, slot_ids, keep_mask)
    branch_b = reduce_rows(jnp.sum(gates[:, :, None] * route_out, axis=1))
    block_out = (resid_b + branch_b).astype(jnp.bfloat16)
    grad_out = out_grad.astype(jnp.float32)
    grad_group = share_rows(out_grad).astype(jnp.float32)
    route_grad = (gates[:, :, None] * grad_group[:, None, :]).astype(jnp.bfloat16)
    grad_gate = jnp.sum(grad_group[:, None, :] * route_out, axis=-1)
    padded_grad = jnp.concatenate(
        [route_grad.reshape(-1, width), jnp.zeros((1, width), jnp.bfloat16)], 0
    )
    grad_sent = jnp.take(padded_grad, table, axis=0).reshape(experts, slots, width)
    grad_result = send_out(grad_sent).reshape(-1, width)
    grad_active = lax.dot_general(
        grad_result, shrink_here, contract_cols, preferred_element_type=jnp.float32
    )
    grad_shrink = lax.dot_general(
        active, grad_result, contract_rows, preferred_element_type=jnp.float32
    )
    gelu_value, gelu_pull = jax.vjp(jax.nn.gelu, inner)
    grad_inner = gelu_pull(grad_active)[0].astype(jnp.bfloat16)
    grad_expand = lax.dot_general(
        arrived, grad_inner, contract_rows, preferred_element_type=jnp.float32
    )
    grad_arrived = lax.dot_general(
        grad_inner, expand_here, contract_cols, preferred_element_type=jnp.float32
    ).astype(jnp.bfloat16)
    grad_routes = bring_back(
        grad_arrived.reshape(experts, slots, width), expert_ids, slot_ids, keep_mask
    )
    grad_pick = keep_float * grad_gate
    grad_chosen = pick * (grad_pick - jnp.sum(pick * grad_pick, axis=-1, keepdims=True))
    grad_logits = jnp.sum(jnp.where(onehot, grad_chosen[:, :, None], 0.0), axis=1)
    router_float = router_full.astype(jnp.float32)
    grad_router = lax.dot_general(
        group_b.astype(jnp.float32), grad_logits, contract_rows, precision=highest
    )
    grad_normed_b = jnp.sum(grad_routes, axis=1) + lax.dot_general(
        grad_logits, router_float, contract_cols, precision=highest
    )
    grad_normed_b = reduce_rows(grad_normed_b)
    norm_value_b, norm_pull_b = jax.vjp(norm_rows, resid_b, gain_b, shift_b)
    grad_resid_b, grad_gain_b, grad_shift_b = norm_pull_b(grad_normed_b)
    grad_resid_b = grad_resid_b + grad_out
    grad_branch = share_rows(grad_resid_b.astype(jnp.bfloat16))
    grad_mix = lax.dot_general(
        grad_branch, heads_out, contract_rows, preferred_element_type=jnp.float32
    )
    grad_heads = jnp.dot(grad_branch, mix_full, preferred_element_type=jnp.float32).astype(
        jnp.bfloat16
    )
    grad_mixed = attend_back(mixed, log_total, grad_heads, images, DH).astype(jnp.bfloat16)
    grad_qkv = jnp.einsum("rd,rcf->dcf", group_a, grad_mixed, preferred_element_type=jnp.float32)
    grad_normed_a = reduce_rows(
        jnp.einsum("rcf,dcf->rd", grad_mixed, qkv_full, preferred_element_type=jnp.float32)
    )
    norm_value_a, norm_pull_a = jax.vjp(norm_rows, resid, gain_a, shift_a)
    grad_resid_a, grad_gain_a, grad_shift_a = norm_pull_a(grad_normed_a)
    grad_tokens = grad_resid_a + grad_resid_b
    summed_weights = (
        lax.psum_scatter(grad_qkv, "dp", scatter_dimension=0, tiled=True),
        lax.psum_scatter(grad_mix, "dp", scatter_dimension=0, tiled=True),
    )
    summed_small = (
        lax.psum_scatter(grad_router, ("dp", "tensor"), scatter_dimension=0, tiled=True),
        lax.psum_scatter(grad_gain_a, ("dp", "tensor"), scatter_dimension=0, tiled=True),
        lax.psum_scatter(grad_shift_a, ("dp", "tensor"), scatter_dimension=0, tiled=True),
        lax.psum_scatter(grad_gain_b, ("dp", "tensor"), scatter_dimension=0, tiled=True),
        lax.psum_scatter(grad_shift_b, ("dp", "tensor"), scatter_dimension=0, tiled=True),
    )
    return (
        block_out,
        grad_tokens,
        summed_weights[0],
        summed_weights[1],
        summed_small[0],
        summed_small[1],
        summed_small[2],
        summed_small[3],
        summed_small[4],
        grad_expand[None],
        grad_shrink[None],
    )


def solution(mesh):
    placed = (
        P(("dp", "tensor"), None),
        P("dp", None, "tensor"),
        P("dp", "tensor"),
        P("dp", None),
        P("dp"),
        P("dp"),
        P("dp"),
        P("dp"),
        P("dp", None, "tensor"),
        P("dp", "tensor", None),
        P("dp", None),
        P("dp", None),
        P("dp", None),
        P(("dp", "tensor"), None),
    )
    return jax.shard_map(
        body,
        mesh=mesh,
        in_specs=placed,
        out_specs=(
            P(("dp", "tensor"), None),
            P(("dp", "tensor"), None),
            P("dp", None, "tensor"),
            P("dp", "tensor"),
            P(("dp", "tensor"), None),
            P(("dp", "tensor")),
            P(("dp", "tensor")),
            P(("dp", "tensor")),
            P(("dp", "tensor")),
            P("dp", None, "tensor"),
            P("dp", "tensor", None),
        ),
        check_vma=False,
    )
```

profile of v0, /device:TPU:0, one launch (start us, length us, event | category | flops | bytes accessed | tf_op | source)
XLA Modules:
  0.0 587.7 jit_solution(10345280353186968672)
XLA Ops:
  13.2 36.4 %all-reduce.22 = (bf16[768]{0:T(1024)(128)(2,1)}, bf16[768]{0:T(1024)(128)(2,1)}, bf16[768]{0:T(1024)(128)(2,1)S(1)}, bf16[768]{0:T(1024)(128)(2,1)S(1)}) all-reduce(bf16[768]{0:T(1024)(128)(2,1)S(1)} %dynamic-update-slice.3, bf16[768]{0:T(1024)(128)(2,1)S(1)} %dynamic-update-slice.2, ...), channel_id=1, replica_groups=mesh['dp'=16,'tensor'=2] {'dp'}, use_global_device_ids=true, to_apply=%add.7 | all-reduce | flops 3072 | bytes 12288
  50.7 5.3 scatter_custom_fusion
  59.6 7.5 %all-gather = bf16[2,197,768]{2,1,0:T(8,128)(2,1)S(1)} all-gather(bf16[1,197,768]{2,1,0:T(8,128)(2,1)S(1)} %fusion.65), channel_id=1, replica_groups=mesh['dp'=16,'tensor'=2] {'tensor'}, dimensions={0}, use_global_device_ids=true | all-gather | bytes 907776 | tf_op jit(solution)/shard_map/all_gather | solution.py:29
  68.1 20.3 %all_gather.37 = bf16[768,384]{1,0:T(8,128)(2,1)} all-gather(bf16[48,384]{1,0:T(8,128)(2,1)S(1)} %copy-done.31), channel_id=1, replica_groups=mesh['dp'=16,'tensor'=2] {'dp'}, dimensions={0}, use_global_device_ids=true | all-gather | bytes 626688 | tf_op jit(solution)/shard_map/all_gather | solution.py:19
  88.4 3.6 convolution_convert_fusion
  92.0 3.9 reshape.321
  95.9 3.2 fusion.86
  100.6 1.6 copy.126
  102.2 2.4 copy.128
  104.6 1.5 multiply_reduce_fusion.3
  108.3 2.6 convolution_convert_fusion.1
  110.9 13.1 %fusion = bf16[200,768]{1,0:T(8,128)(2,1)S(1)} fusion(bf16[394,768]{1,0:T(8,128)(2,1)} %convolution_convert_fusion.1), kind=kCustom, calls=%all-reduce-scatter | all-reduce-scatter fusion | flops 307201 | bytes 912896
  124.1 2.5 collective-permute-start
  129.2 8.9 %all-gather.1 = bf16[2,197,768]{2,1,0:T(8,128)(2,1)} all-gather(bf16[1,197,768]{2,1,0:T(8,128)(2,1)S(1)} %fusion.64), channel_id=1, replica_groups=mesh['dp'=16,'tensor'=2] {'tensor'}, dimensions={0}, use_global_device_ids=true | all-gather | bytes 907776 | tf_op jit(solution)/shard_map/all_gather | solution.py:29
  138.1 2.0 reshape.289
  141.2 5.2 gather_fusion
  146.5 1.8 broadcast_select_fusion.1
  148.2 39.5 %all_to_all.20 = bf16[16,64,768]{2,1,0:T(8,128)(2,1)S(1)} all-to-all(bf16[16,64,768]{2,1,0:T(8,128)(2,1)S(1)} %broadcast_select_fusion.1), channel_id=1, replica_groups=mesh['dp'=16,'tensor'=2] {'dp'}, dimensions={0} | all-to-all | bytes 3145728 | tf_op jit(solution)/shard_map/all_to_all | solution.py:39
  188.9 2.6 fusion.19
  191.5 4.8 fusion.24
  196.4 5.2 all-to-all-start.1
  201.8 42.1 %all-gather.2 = bf16[16,48,16]{1,2,0:T(8,128)(2,1)S(1)} all-gather(bf16[1,48,16]{1,2,0:T(8,128)(2,1)S(1)} %bitcast.127), channel_id=1, replica_groups=mesh['dp'=16,'tensor'=2] {'dp'}, dimensions={0}, use_global_device_ids=true | all-gather | bytes 26112 | tf_op jit(solution)/shard_map/all_gather | solution.py:20
  244.0 10.3 %all-gather.3 = bf16[2,197,768]{2,1,0:T(8,128)(2,1)} all-gather(bf16[1,197,768]{2,1,0:T(8,128)(2,1)S(1)} %bitcast.122), channel_id=1, replica_groups=mesh['dp'=16,'tensor'=2] {'tensor'}, dimensions={0}, use_global_device_ids=true | all-gather | bytes 907776 | tf_op jit(solution)/shard_map/all_gather | solution.py:29
  254.3 2.2 reshape.296
  256.5 3.6 mul.256
  260.1 4.2 mul.257
  264.7 2.7 concatenate.15
  267.4 6.4 %gather_fusion.2 = bf16[788,768]{1,0:T(8,128)(2,1)} fusion(bf16[1025,768]{1,0:T(8,128)(2,1)} %concatenate.15, s32[1024]{0:T(1024)S(1)} %pad_clamp_fusion), kind=kCustom, calls=%fused_computation.clone | custom fusion | bytes 2423888 | tf_op jit(solution)/shard_map/jit(_take)/gather | solution.py:46
  273.7 2.6 multiply_reduce_fusion.1
  277.0 1.9 multiply_convert_fusion.2
  280.0 7.0 %gather_fusion.1 = bf16[1024,768]{1,0:T(8,128)(2,1)} fusion(bf16[789,768]{1,0:T(8,128)(2,1)} %concatenate.16, s32[1024]{0:T(1024)S(1)} %get-tuple-element.44), kind=kCustom, calls=%fused_computation.3 | custom fusion | bytes 3149824 | tf_op jit(solution)/shard_map/jit(_take)/gather | solution.py:184
  287.0 1.6 broadcast_select_fusion
  288.6 55.6 %all_to_all.21 = bf16[16,64,768]{2,1,0:T(8,128)(2,1)S(1)} all-to-all(bf16[16,64,768]{2,1,0:T(8,128)(2,1)S(1)} %broadcast_select_fusion), channel_id=1, replica_groups=mesh['dp'=16,'tensor'=2] {'dp'}, dimensions={0} | all-to-all | bytes 3145728 | tf_op jit(solution)/shard_map/all_to_all | solution.py:39
  344.2 8.3 %fusion.10 = bf16[1024,1536]{1,0:T(8,128)(2,1)S(1)} fusion(f32[1024,1536]{1,0:T(8,128)} %copy-done.49, bf16[1024,768]{1,0:T(8,128)(2,1)S(1)} %bitcast.123, bf16[1,1536,768]{2,1,0:T(8,128)(2,1)S(1)} %copy-done), kind=kOutput, calls=%fused_computation.13 | convolution fusion | flops 2447376384 | bytes 13369344 | tf_op jit(solution)/shard_map/dot_general | solution.py:186
  352.5 3.7 fusion.21
  356.2 5.0 all-to-all-start.3
  361.3 31.9 %all-to-all-done.3 = bf16[16,64,768]{2,1,0:T(8,128)(2,1)S(1)} async-done(((bf16[16,64,768]{2,1,0:T(8,128)(2,1)}), bf16[16,64,768]{2,1,0:T(8,128)(2,1)S(1)}, u32[]{:S(2)}, u32[]{:S(2)}) %all-to-all-start.3) | async-done | bytes 1572896 | tf_op jit(solution)/shard_map/all_to_all | solution.py:54
  394.4 1.5 concatenate.17
  395.9 4.1 gather_fusion.3
  400.0 4.3 select_convert_fusion
  404.2 4.0 reshape.229
  408.3 4.6 reduce_sum.202
  413.5 12.9 %fusion.2 = bf16[200,768]{1,0:T(8,128)(2,1)S(1)} fusion(bf16[394,768]{1,0:T(8,128)(2,1)S(1)} %fusion.29), kind=kCustom, calls=%all-reduce-scatter.2 | all-reduce-scatter fusion | flops 307201 | bytes 912896
  426.5 2.5 collective-permute-start.2
  432.7 9.1 %all-gather.4 = bf16[2,197,768]{2,1,0:T(8,128)(2,1)S(1)} all-gather(bf16[1,197,768]{2,1,0:T(8,128)(2,1)S(1)} %fusion.63), channel_id=1, replica_groups=mesh['dp'=16,'tensor'=2] {'tensor'}, dimensions={0}, use_global_device_ids=true | all-gather | bytes 907776 | tf_op jit(solution)/shard_map/all_gather | solution.py:29
  442.7 1.7 convolution_convert_fusion.4
  444.4 2.8 fusion.89
  448.2 4.0 multiply_reduce_fusion
  453.8 3.0 multiply_convert_fusion.1
  457.9 2.3 copy.114
  460.3 2.6 reshape.312
  467.2 3.1 fusion.88
  471.9 8.7 %convolution_bitcast_fusion = f32[1,1536,768]{2,1,0:T(8,128)} fusion(bf16[1024,768]{1,0:T(8,128)(2,1)S(1)} %bitcast.124, f32[1024,1536]{1,0:T(8,128)} %copy-done.49), kind=kOutput, calls=%fused_computation.15 | convolution fusion | flops 2430074880 | bytes 12582912 | tf_op jit(solution)/shard_map/dot_general | solution.py:189
  480.6 4.0 reshape.228
  484.6 4.9 multiply_reduce_fusion.2
  489.5 1.8 fusion.28
  491.3 17.0 %fusion.83 = (bf16[200,768]{1,0:T(8,128)(2,1)S(1)}, bf16[200,768]{1,0:T(8,128)(2,1)}) fusion(bf16[394,768]{1,0:T(8,128)(2,1)S(1)} %multiply_reduce_fusion.2, bf16[394,768]{1,0:T(8,128)(2,1)} %fusion.28), kind=kCustom, calls=%all-reduce-scatter.4 | all-reduce-scatter fusion | flops 614401 | bytes 1825280
  509.1 3.4 collective-permute-start.3
  512.5 6.4 %convolution_bitcast_fusion.1 = f32[1,768,1536]{2,1,0:T(8,128)} fusion(bf16[1024,768]{1,0:T(8,128)(2,1)S(1)} %bitcast.118, bf16[1024,1536]{1,0:T(8,128)(2,1)} %copy-done.20), kind=kOutput, calls=%fused_computation.16 | convolution fusion | flops 2415919104 | bytes 9437184 | tf_op jit(solution)/shard_map/dot_general | solution.py:194
  520.2 2.2 concatenate.21
  523.3 44.1 %all-reduce.21 = (f32[768,16]{0,1:T(8,128)S(1)}, f32[768]{0:T(1024)S(1)}, f32[768]{0:T(1024)S(1)}, f32[768]{0:T(1024)S(1)}, f32[768]{0:T(1024)S(1)}) all-reduce(f32[768,16]{0,1:T(8,128)S(1)} %fusion.90, f32[768]{0:T(1024)S(1)} %get-tuple-element.14, ...), channel_id=8, replica_groups=mesh['dp'=16,'tensor'=2] {'dp','tensor'}, use_global_device_ids=true, to_apply=%region_26.28.clone | all-reduce | flops 15360 | bytes 122880
  569.7 3.3 concatenate.19
  573.7 2.7 add_add_fusion.2
  576.3 4.4 reduce-scatter.12.cloned.1.call-done
  (207 shorter events, 42.9 us)
Async XLA Ops:
  7.2 184.4 %copy-start = (bf16[1,1536,768]{2,1,0:T(8,128)(2,1)S(1)}, bf16[1,1536,768]{2,1,0:T(8,128)(2,1)}, u32[]{:S(2)}) copy-start(bf16[1,1536,768]{2,1,0:T(8,128)(2,1)} %param.25) | copy-start | bytes 7077892
  7.2 60.9 %copy-start.31 = (bf16[48,384]{1,0:T(8,128)(2,1)S(1)}, bf16[48,384]{1,0:T(8,128)(2,1)}, u32[]{:S(2)}) copy-start(bf16[48,384]{1,0:T(8,128)(2,1)} %param.18) | copy-start | bytes 110596
  7.2 81.2 %all-gather.7.cloned.1.call-start = ((), (), s32[]{:S(2)}) async-start(), calls=%async_computation.6 | async-start | bytes 1880064 | tf_op jit(solution)/shard_map/all_gather | solution.py:18
  50.5 41.5 %copy-start.24 = (s32[394,2]{1,0:T(8,128)}, s32[394,2]{1,0:T(8,128)S(1)}, u32[]{:S(2)}) copy-start(s32[394,2]{1,0:T(8,128)S(1)} %copy.94) | copy-start | bytes 9460
  58.4 33.6 %copy-start.38 = (f32[197]{0:T(256)}, f32[197]{0:T(256)S(1)}, u32[]{:S(2)}) copy-start(f32[197]{0:T(256)S(1)} %fusion.47) | copy-start | bytes 2368
  58.4 33.6 %copy-start.34 = (f32[197]{0:T(256)}, f32[197]{0:T(256)S(1)}, u32[]{:S(2)}) copy-start(f32[197]{0:T(256)S(1)} %fusion.79) | copy-start | bytes 2368
  100.6 5.6 copy-start.15
  102.2 4.5 copy-start.13
  106.2 1.4 copy-start.2
  107.6 18.9 %copy-start.45 = (u32[32]{0:T(128)S(1)}, u32[32]{0:T(128)}, u32[]{:S(2)}) copy-start(u32[32]{0:T(128)} %constant.139) | copy-start | bytes 388
  107.7 20.2 %copy-start.44 = (bf16[768]{0:T(1024)(128)(2,1)S(1)}, bf16[768]{0:T(1024)(128)(2,1)}, u32[]{:S(2)}) copy-start(bf16[768]{0:T(1024)(128)(2,1)} %get-tuple-element.23) | copy-start | bytes 4612
  107.7 20.2 %copy-start.43 = (bf16[768]{0:T(1024)(128)(2,1)S(1)}, bf16[768]{0:T(1024)(128)(2,1)}, u32[]{:S(2)}) copy-start(bf16[768]{0:T(1024)(128)(2,1)} %get-tuple-element.24) | copy-start | bytes 4612
  107.7 20.8 %copy-start.4 = (bf16[197,768]{1,0:T(8,128)(2,1)S(1)}, bf16[197,768]{1,0:T(8,128)(2,1)}, u32[]{:S(2)}) copy-start(bf16[197,768]{1,0:T(8,128)(2,1)} %param.16) | copy-start | bytes 907780
  108.3 19.6 %copy-start.18 = (bf16[394,384]{0,1:T(8,128)(2,1)}, bf16[394,384]{0,1:T(8,128)(2,1)S(1)}, u32[]{:S(2)}) copy-start(bf16[394,384]{0,1:T(8,128)(2,1)S(1)} %convert_element_type.124) | copy-start | bytes 907780
  124.1 3.8 collective-permute-start
  128.4 9.6 %copy-start.5 = (bf16[203,768]{1,0:T(8,128)(2,1)}, bf16[203,768]{1,0:T(8,128)(2,1)S(1)}, u32[]{:S(2)}) copy-start(bf16[203,768]{1,0:T(8,128)(2,1)S(1)} %concatenate.18) | copy-start | bytes 935428
  146.5 42.5 %copy-start.46 = (bf16[1,768,1536]{2,1,0:T(8,128)(2,1)S(1)}, bf16[1,768,1536]{2,1,0:T(8,128)(2,1)}, u32[]{:S(2)}) copy-start(bf16[1,768,1536]{2,1,0:T(8,128)(2,1)} %param.24) | copy-start | bytes 7077892
  187.8 1.2 copy-start.9
  191.5 4.8 copy-start.49
  196.4 5.2 copy-start.25
  196.4 5.4 copy-start.42
  196.4 47.6 %copy-start.21 = (bf16[197,768]{1,0:T(8,128)(2,1)S(1)}, bf16[197,768]{1,0:T(8,128)(2,1)}, u32[]{:S(2)}) copy-start(bf16[197,768]{1,0:T(8,128)(2,1)} %param.29) | copy-start | bytes 907780
  196.4 68.3 %all-to-all-start.1 = ((bf16[16,64,768]{2,1,0:T(8,128)(2,1)}), bf16[16,64,768]{2,1,0:T(8,128)(2,1)}, u32[]{:S(2)}, u32[]{:S(2)}) async-start(bf16[16,64,768]{2,1,0:T(8,128)(2,1)} %bitcast.125), calls=%async_computation.1 | async-start | bytes 3145728 | tf_op jit(solution)/shard_map/all_to_all | solution.py:54
  260.1 4.2 copy-start.7
  260.1 4.5 copy-start.32
  273.7 2.9 copy-start.33
  344.2 8.3 %copy-start.28 = (bf16[16,64,768]{2,1,0:T(8,128)(2,1)}, bf16[16,64,768]{2,1,0:T(8,128)(2,1)S(1)}, u32[]{:S(2)}) copy-start(bf16[16,64,768]{2,1,0:T(8,128)(2,1)S(1)} %all_to_all.21) | copy-start | bytes 4718596
  344.2 8.3 %copy-start.47 = (bf16[1,768,1536]{2,1,0:T(8,128)(2,1)S(1)}, bf16[1,768,1536]{2,1,0:T(8,128)(2,1)}, u32[]{:S(2)}) copy-start(bf16[1,768,1536]{2,1,0:T(8,128)(2,1)} %param.24) | copy-start | bytes 7077892
  352.5 3.7 copy-start.20
  356.2 37.0 %all-to-all-start.3 = ((bf16[16,64,768]{2,1,0:T(8,128)(2,1)}), bf16[16,64,768]{2,1,0:T(8,128)(2,1)S(1)}, u32[]{:S(2)}, u32[]{:S(2)}) async-start(bf16[16,64,768]{2,1,0:T(8,128)(2,1)} %bitcast.126), calls=%async_computation.3 | async-start | bytes 3145728 | tf_op jit(solution)/shard_map/all_to_all | solution.py:54
  361.3 215.1 %reduce-scatter.14.cloned.1.call-start = ((), (), s32[]{:S(2)}) async-start(), calls=%async_computation.8 | async-start | bytes 1253376 | tf_op jit(solution)/shard_map/reduce_scatter | solution.py:234
  393.3 1.1 copy-start.11
  412.8 18.0 %copy-start.6 = (bf16[203,768]{1,0:T(8,128)(2,1)S(1)}, bf16[203,768]{1,0:T(8,128)(2,1)}, u32[]{:S(2)}) copy-start(bf16[203,768]{1,0:T(8,128)(2,1)} %copy-done.5) | copy-start | bytes 935428
  413.5 19.0 %copy-start.22 = (bf16[197,768]{1,0:T(8,128)(2,1)S(1)}, bf16[197,768]{1,0:T(8,128)(2,1)}, u32[]{:S(2)}) copy-start(bf16[197,768]{1,0:T(8,128)(2,1)} %param.29) | copy-start | bytes 907780
  426.5 3.9 collective-permute-start.2
  432.5 14.7 %copy-start.12 = (f32[197,768]{1,0:T(8,128)}, f32[197,768]{1,0:T(8,128)S(1)}, u32[]{:S(2)}) copy-start(f32[197,768]{1,0:T(8,128)S(1)} %get-tuple-element.32) | copy-start | bytes 1815556
  432.5 12.0 %copy-start.19 = (bf16[394,384]{0,1:T(8,128)(2,1)S(1)}, bf16[394,384]{0,1:T(8,128)(2,1)}, u32[]{:S(2)}) copy-start(bf16[394,384]{0,1:T(8,128)(2,1)} %copy-done.18) | copy-start | bytes 907780
  432.5 14.7 %copy-start.40 = (f32[197]{0:T(256)}, f32[197]{0:T(256)S(1)}, u32[]{:S(2)}) copy-start(f32[197]{0:T(256)S(1)} %negate_multiply_fusion.1) | copy-start | bytes 2368
  444.4 3.8 copy-start.14
  447.2 133.5 %reduce-scatter.12.cloned.1.call-start = ((), (), s32[]{:S(2)}) async-start(), calls=%async_computation.7 | async-start | bytes 3760128 | tf_op jit(solution)/shard_map/reduce_scatter | solution.py:233
  448.2 4.0 copy-start.3
  453.8 3.0 copy-start.17
  456.8 6.0 %copy-start.16 = (bf16[2,197,1,6,64]{1,4,3,0,2:T(8,128)(2,1)S(1)}, bf16[2,197,1,6,64]{1,4,3,0,2:T(8,128)(2,1)}, u32[]{:S(2)}) copy-start(bf16[2,197,1,6,64]{1,4,3,0,2:T(8,128)(2,1)} %copy-done.15) | copy-start | bytes 907780
  463.3 3.9 copy-start.23
  467.2 3.1 copy-start.26
  470.3 1.1 copy-start.8
  470.3 1.6 copy-start.29
  484.6 4.9 copy-start.27
  484.6 4.9 copy-start.48
  489.5 23.0 %copy-start.10 = (bf16[16,64,768]{2,1,0:T(8,128)(2,1)S(1)}, bf16[16,64,768]{2,1,0:T(8,128)(2,1)}, u32[]{:S(2)}) copy-start(bf16[16,64,768]{2,1,0:T(8,128)(2,1)} %copy-done.9) | copy-start | bytes 4718596
  508.3 10.6 %copy-start.30 = (bf16[200,768]{1,0:T(8,128)(2,1)}, bf16[200,768]{1,0:T(8,128)(2,1)S(1)}, u32[]{:S(2)}) copy-start(bf16[200,768]{1,0:T(8,128)(2,1)S(1)} %get-tuple-element.29) | copy-start | bytes 921604
  509.0 13.8 %copy-start.39 = (f32[197]{0:T(256)S(1)}, f32[197]{0:T(256)}, u32[]{:S(2)}) copy-start(f32[197]{0:T(256)} %copy-done.38) | copy-start | bytes 2368
  509.0 13.8 %copy-start.35 = (f32[197]{0:T(256)S(1)}, f32[197]{0:T(256)}, u32[]{:S(2)}) copy-start(f32[197]{0:T(256)} %copy-done.34) | copy-start | bytes 2368
  509.0 14.2 %copy-start.36 = (f32[768]{0:T(1024)S(1)}, f32[768]{0:T(1024)}, u32[]{:S(2)}) copy-start(f32[768]{0:T(1024)} %get-tuple-element.12) | copy-start | bytes 9220
  509.0 14.2 %copy-start.37 = (f32[768]{0:T(1024)S(1)}, f32[768]{0:T(1024)}, u32[]{:S(2)}) copy-start(f32[768]{0:T(1024)} %get-tuple-element.16) | copy-start | bytes 9220
  509.1 11.1 %collective-permute-start.3 = (bf16[3,768]{1,0:T(4,128)(2,1)S(1)}, bf16[3,768]{1,0:T(4,128)(2,1)S(1)}, u32[]{:S(2)}, u32[]{:S(2)}) collective-permute-start(bf16[3,768]{1,0:T(4,128)(2,1)S(1)} %slice.37), channel_id=1, source_target_pairs={{0,1},{2,3},{4,5},{6,7},{8,9},{10,11},{12,13},{14,15},{16,17},{18,... | collective-permute-start | bytes 13832
  518.9 54.8 %copy-start.41 = (f32[197]{0:T(256)S(1)}, f32[197]{0:T(256)}, u32[]{:S(2)}) copy-start(f32[197]{0:T(256)} %copy-done.40) | copy-start | bytes 2368
  518.9 50.8 %collective-permute-start.1 = (bf16[3,768]{1,0:T(4,128)(2,1)S(1)}, bf16[3,768]{1,0:T(4,128)(2,1)S(1)}, u32[]{:S(2)}, u32[]{:S(2)}) collective-permute-start(bf16[3,768]{1,0:T(4,128)(2,1)S(1)} %slice.35), channel_id=1, source_target_pairs={{0,1},{2,3},{4,5},{6,7},{8,9},{10,11},{12,13},{14,15},{16,17},{18,... | collective-permute-start | bytes 13832
  520.2 60.5 %copy-start.1 = (bf16[1,1536,768]{2,1,0:T(8,128)(2,1)S(1)}, bf16[1,1536,768]{2,1,0:T(8,128)(2,1)}, u32[]{:S(2)}) copy-start(bf16[1,1536,768]{2,1,0:T(8,128)(2,1)} %param.25) | copy-start | bytes 7077892
Sparse Core Ops, SparseCore 0:
  10.4 43.3 all-gather.6
  447.4 61.6 reduce-scatter.13
  513.5 67.1 reduce-scatter.11
where the time goes:
time: 598 us; the launch traced here: 588 us
  blocking collectives  317 us (53%)
  local copies, waits for them, and re-layouts  101 us (17%)
  matrix products  59.6 us (10%)
  waiting for transfers between devices  38.4 us (6%)
  other arithmetic  35.4 us (6%)
  starting transfers between devices  20.1 us (3%)
  between operations  16.5 us (3%)
    unnamed x5, blocking collectives  123 us
    all_to_all x2, blocking collectives, send_out(): return lax.all_to_all(buffer, 'dp', split_axis=0, concat_axis=0, tiled=True)  95.1 us
    all_gather x1, blocking collectives, fetch(): lax.all_gather(shards[2], 'dp', axis=0, tiled=True)  42.1 us
    all_gather x4, blocking collectives, share_rows(): return lax.all_gather(values, 'tensor', axis=0, tiled=True)  35.8 us
    all_to_all x2, waiting for transfers between devices, bring_back(): lax.all_to_all(values, 'dp', split_axis=0, concat_axis=0, tiled=True)  31.9 us
    unnamed x132, local copies, waits for them, and re-layouts  31.1 us
    all_gather x1, blocking collectives, fetch(): lax.all_gather(shards[1], 'dp', axis=0, tiled=True)  20.3 us
  transfers between devices with their start and end apart: 9, of which 3 were waited for; matrix products, arithmetic and copies ran while one was open for 18% of the time, Pallas kernels for 0%

commit v1 on v0

--- a/solution.py
+++ b/solution.py
@@ -1,3 +1,4 @@
+import functools
 import jax
 import jax.numpy as jnp
 from jax import lax
@@ -7,6 +8,33 @@
 SEQ = 197
 
 
+def choose_windows_by_axis(payload, array_dim):
+    state_next = list(payload.shape[1:])
+    state_next[array_dim] *= payload.shape[0]
+    return jnp.moveaxis(payload, 0, array_dim).reshape(state_next)
+
+
+def set_sector_over_axis(field, shard_axis, k_dim):
+    nodes = lax.axis_size(shard_axis)
+    buffers = [(no, (no + 1) % nodes) for no in range(nodes)]
+    rack = [(dd, u) for u, dd in buffers]
+    tile_out, low = ([], [])
+    for pp in range(nodes - 1):
+        if pp % 2 == 0:
+            tile_out.append(lax.ppermute(tile_out[-1] if tile_out else field, shard_axis, buffers))
+        else:
+            far_arr = lax.ppermute(low[-1] if low else field, shard_axis, rack)
+            low.append(far_arr)
+    found_now = jnp.stack([*tile_out[::-1], field, *low], axis=0)
+    t1 = lax.axis_index(shard_axis)
+    h_now = t1 - len(tile_out)
+    found_now = found_now[(jnp.arange(nodes) - h_now) % nodes]
+    return choose_windows_by_axis(found_now, k_dim)
+
+
+track_the_frames = functools.partial(set_sector_over_axis, shard_axis="dp", k_dim=0)
+
+
 def norm_rows(values, gain, shift):
     centre = values - jnp.mean(values, axis=-1, keepdims=True)
     spread = jnp.mean(centre * centre, axis=-1, keepdims=True)
@@ -17,7 +45,7 @@
     return (
         lax.all_gather(shards[0], "dp", axis=0, tiled=True),
         lax.all_gather(shards[1], "dp", axis=0, tiled=True),
-        lax.all_gather(shards[2], "dp", axis=0, tiled=True),
+        track_the_frames(shards[2]),
         lax.all_gather(shards[3], "dp", axis=0, tiled=True),
         lax.all_gather(shards[4], "dp", axis=0, tiled=True),
         lax.all_gather(shards[5], "dp", axis=0, tiled=True),

time: 598 us -> 619 us (1.035)
  blocking collectives: 317 us -> 233 us
  waiting for transfers between devices: 38.4 us -> 106 us
  starting transfers between devices: 20.1 us -> 54.7 us
    all_gather x1 -> x0, blocking collectives: 42.1 us -> none  [fetch(): lax.all_gather(shards[2], 'dp', axis=0, tiled=True)]
    all_to_all x2 -> x1, blocking collectives: 95.1 us -> 56.2 us  [send_out(): return lax.all_to_all(buffer, 'dp', split_axis=0, concat_axis=0, tiled=True)]
    ppermute x0 -> x15, waiting for transfers between devices: none -> 36.8 us  [the longest x8 34.2 us: set_sector_over_axis(): lax.ppermute(tile_out[-1] if tile_out else field, shard_axis, buffers)]
    all_to_all x2, waiting for transfers between devices: 31.9 us -> 62.6 us  [bring_back(): lax.all_to_all(values, 'dp', split_axis=0, concat_axis=0, tiled=True)]
    ppermute x0 -> x15, starting transfers between devices: none -> 30.4 us  [the longest x7 30.1 us: set_sector_over_axis(): far_arr = lax.ppermute(low[-1] if low else field, shard_axis, rack)]
    unnamed x132 -> x134, local copies, waits for them, and re-layouts: 31.1 us -> 29.1 us
  transfers between devices with their start and end apart: 9 -> 25, of which waited for: 3 -> 10; matrix products, arithmetic and copies ran while one was open for 18% -> 19% of each run, Pallas kernels for 0% -> 0%
where the time goes in v1:
time: 619 us; the launch traced here: 609 us
  blocking collectives  233 us (38%)
  waiting for transfers between devices  106 us (17%)
  local copies, waits for them, and re-layouts  99.5 us (16%)
  matrix products  62.9 us (10%)
  starting transfers between devices  54.7 us (9%)
  other arithmetic  36.5 us (6%)
  between operations  16.6 us (3%)
    unnamed x5, blocking collectives  123 us
    all_to_all x2, waiting for transfers between devices, bring_back(): lax.all_to_all(values, 'dp', split_axis=0, concat_axis=0, tiled=True)  62.6 us
    all_to_all x1, blocking collectives, send_out(): return lax.all_to_all(buffer, 'dp', split_axis=0, concat_axis=0, tiled=True)  56.2 us
    ppermute x8, waiting for transfers between devices, set_sector_over_axis(): lax.ppermute(tile_out[-1] if tile_out else field, shard_axis, buffers)  34.2 us
    all_gather x4, blocking collectives, share_rows(): return lax.all_gather(values, 'tensor', axis=0, tiled=True)  33.1 us
    ppermute x7, starting transfers between devices, set_sector_over_axis(): far_arr = lax.ppermute(low[-1] if low else field, shard_axis, rack)  30.1 us
    unnamed x134, local copies, waits for them, and re-layouts  29.1 us
    all_gather x1, blocking collectives, fetch(): lax.all_gather(shards[1], 'dp', axis=0, tiled=True)  20.3 us
  transfers between devices with their start and end apart: 25, of which 10 were waited for; matrix products, arithmetic and copies ran while one was open for 19% of the time, Pallas kernels for 0%

profile of v1, /device:TPU:0, one launch (start us, length us, event | category | flops | bytes accessed | tf_op | source)
XLA Modules:
  0.0 608.6 jit_solution(13231222664455072434)
XLA Ops:
  13.2 36.4 %all-reduce.22 = (bf16[768]{0:T(1024)(128)(2,1)}, bf16[768]{0:T(1024)(128)(2,1)S(1)}, bf16[768]{0:T(1024)(128)(2,1)S(1)}, bf16[768]{0:T(1024)(128)(2,1)S(1)}) all-reduce(bf16[768]{0:T(1024)(128)(2,1)S(1)} %dynamic-update-slice.3, bf16[768]{0:T(1024)(128)(2,1)S(1)} %dynamic-update-slice.2, ...), channel_id=1, replica_groups=mesh['dp'=16,'tensor'=2] {'dp'}, use_global_device_ids=true, to_apply=%add.7 | all-reduce | flops 3072 | bytes 12288
  50.7 5.3 scatter_custom_fusion
  59.6 7.5 %all-gather = bf16[2,197,768]{2,1,0:T(8,128)(2,1)S(1)} all-gather(bf16[1,197,768]{2,1,0:T(8,128)(2,1)S(1)} %fusion.65), channel_id=1, replica_groups=mesh['dp'=16,'tensor'=2] {'tensor'}, dimensions={0}, use_global_device_ids=true | all-gather | bytes 907776 | tf_op jit(solution)/shard_map/all_gather | solution.py:57
  68.1 20.3 %all_gather.34 = bf16[768,384]{1,0:T(8,128)(2,1)} all-gather(bf16[48,384]{1,0:T(8,128)(2,1)S(1)} %copy-done.27), channel_id=1, replica_groups=mesh['dp'=16,'tensor'=2] {'dp'}, dimensions={0}, use_global_device_ids=true | all-gather | bytes 626688 | tf_op jit(solution)/shard_map/all_gather | solution.py:47
  88.4 3.6 convolution_convert_fusion
  92.0 3.9 reshape.380
  95.9 3.2 fusion.88
  102.2 2.4 copy.128
  108.3 2.6 convolution_convert_fusion.1
  110.9 13.2 %fusion = bf16[200,768]{1,0:T(8,128)(2,1)S(1)} fusion(bf16[394,768]{1,0:T(8,128)(2,1)} %convolution_convert_fusion.1), kind=kCustom, calls=%all-reduce-scatter | all-reduce-scatter fusion | flops 307201 | bytes 912896
  124.1 2.5 collective-permute-start.15
  129.2 8.9 %all-gather.1 = bf16[2,197,768]{2,1,0:T(8,128)(2,1)} all-gather(bf16[1,197,768]{2,1,0:T(8,128)(2,1)S(1)} %fusion.64), channel_id=1, replica_groups=mesh['dp'=16,'tensor'=2] {'tensor'}, dimensions={0}, use_global_device_ids=true | all-gather | bytes 907776 | tf_op jit(solution)/shard_map/all_gather | solution.py:57
  141.2 5.2 gather_fusion.1
  146.5 2.8 broadcast_select_fusion.1
  149.3 4.5 all-to-all-start
  154.1 30.7 %collective-permute-done = bf16[48,16]{0,1:T(8,128)(2,1)S(1)} collective-permute-done((bf16[48,16]{0,1:T(8,128)(2,1)S(1)}, bf16[48,16]{0,1:T(8,128)(2,1)S(1)}, u32[]{:S(2)}, u32[]{:S(2)}) %collective-permute-start) | collective-permute-done | bytes 1568 | tf_op jit(solution)/shard_map/ppermute | solution.py:24
  184.8 4.4 collective-permute-start.8
  190.6 4.4 collective-permute-start.9
  196.4 4.7 collective-permute-start.10
  202.1 7.6 %all-gather.2 = bf16[2,197,768]{2,1,0:T(8,128)(2,1)} all-gather(bf16[1,197,768]{2,1,0:T(8,128)(2,1)S(1)} %bitcast.153), channel_id=1, replica_groups=mesh['dp'=16,'tensor'=2] {'tensor'}, dimensions={0}, use_global_device_ids=true | all-gather | bytes 907776 | tf_op jit(solution)/shard_map/all_gather | solution.py:57
  209.7 3.3 collective-permute-start.11
  214.3 4.4 collective-permute-start.12
  220.1 4.4 collective-permute-start.13
  224.5 2.2 reshape.355
  226.7 3.6 mul.256
  230.2 4.1 mul.257
  234.4 4.4 collective-permute-start.14
  238.9 4.7 fusion.19
  243.6 4.8 fusion.24
  248.4 4.5 all-to-all-start.1
  254.2 30.7 %all-to-all-done.1 = bf16[16,64,768]{2,1,0:T(8,128)(2,1)} async-done(((bf16[16,64,768]{2,1,0:T(8,128)(2,1)}), bf16[16,64,768]{2,1,0:T(8,128)(2,1)}, u32[]{:S(2)}, u32[]{:S(2)}) %all-to-all-start.1) | async-done | bytes 1572896 | tf_op jit(solution)/shard_map/all_to_all | solution.py:82
  284.9 2.7 concatenate.15
  287.6 6.4 %gather_fusion.3 = bf16[788,768]{1,0:T(8,128)(2,1)} fusion(bf16[1025,768]{1,0:T(8,128)(2,1)} %concatenate.15, s32[1024]{0:T(1024)S(1)} %pad_clamp_fusion), kind=kCustom, calls=%fused_computation.clone | custom fusion | bytes 2423888 | tf_op jit(solution)/shard_map/jit(_take)/gather | solution.py:74
  294.0 2.6 multiply_reduce_fusion.1
  300.2 7.0 %gather_fusion.2 = bf16[1024,768]{1,0:T(8,128)(2,1)} fusion(bf16[789,768]{1,0:T(8,128)(2,1)} %concatenate.16, s32[1024]{0:T(1024)S(1)} %get-tuple-element.44), kind=kCustom, calls=%fused_computation.4 | custom fusion | bytes 3149824 | tf_op jit(solution)/shard_map/jit(_take)/gather | solution.py:212
  308.9 56.2 %all_to_all.20 = bf16[16,64,768]{2,1,0:T(8,128)(2,1)S(1)} all-to-all(bf16[16,64,768]{2,1,0:T(8,128)(2,1)S(1)} %broadcast_select_fusion), channel_id=1, replica_groups=mesh['dp'=16,'tensor'=2] {'dp'}, dimensions={0} | all-to-all | bytes 3145728 | tf_op jit(solution)/shard_map/all_to_all | solution.py:67
  365.1 8.3 %fusion.10 = bf16[1024,1536]{1,0:T(8,128)(2,1)S(1)} fusion(f32[1024,1536]{1,0:T(8,128)} %copy-done.43, bf16[1024,768]{1,0:T(8,128)(2,1)S(1)} %bitcast.154, bf16[1,1536,768]{2,1,0:T(8,128)(2,1)S(1)} %copy-done), kind=kOutput, calls=%fused_computation.14 | convolution fusion | flops 2447376384 | bytes 13369344 | tf_op jit(solution)/shard_map/dot_general | solution.py:214
  373.4 3.7 fusion.21
  377.1 5.0 all-to-all-start.3
  382.2 31.9 %all-to-all-done.3 = bf16[16,64,768]{2,1,0:T(8,128)(2,1)S(1)} async-done(((bf16[16,64,768]{2,1,0:T(8,128)(2,1)}), bf16[16,64,768]{2,1,0:T(8,128)(2,1)S(1)}, u32[]{:S(2)}, u32[]{:S(2)}) %all-to-all-start.3) | async-done | bytes 1572896 | tf_op jit(solution)/shard_map/all_to_all | solution.py:82
  416.8 4.1 gather_fusion.4
  420.8 4.2 select_convert_fusion
  425.1 4.0 reshape.282
  429.1 4.6 reduce_sum.202
  434.4 12.9 %fusion.2 = bf16[200,768]{1,0:T(8,128)(2,1)S(1)} fusion(bf16[394,768]{1,0:T(8,128)(2,1)S(1)} %fusion.29), kind=kCustom, calls=%all-reduce-scatter.2 | all-reduce-scatter fusion | flops 307201 | bytes 912896
  447.3 2.5 collective-permute-start.17
  453.5 9.1 %all-gather.3 = bf16[2,197,768]{2,1,0:T(8,128)(2,1)S(1)} all-gather(bf16[1,197,768]{2,1,0:T(8,128)(2,1)S(1)} %fusion.63), channel_id=1, replica_groups=mesh['dp'=16,'tensor'=2] {'tensor'}, dimensions={0}, use_global_device_ids=true | all-gather | bytes 907776 | tf_op jit(solution)/shard_map/all_gather | solution.py:57
  465.3 2.8 fusion.91
  469.1 4.0 multiply_reduce_fusion
  474.6 3.0 multiply_convert_fusion.1
  478.8 2.3 copy.114
  481.1 2.6 reshape.371
  488.0 3.1 fusion.90
  492.5 9.1 %convolution_bitcast_fusion = f32[1,1536,768]{2,1,0:T(8,128)} fusion(bf16[1024,768]{1,0:T(8,128)(2,1)} %bitcast.155, f32[1024,1536]{1,0:T(8,128)} %copy-done.43), kind=kOutput, calls=%fused_computation.16 | convolution fusion | flops 2430074880 | bytes 12582912 | tf_op jit(solution)/shard_map/dot_general | solution.py:217
  501.6 4.0 reshape.281
  505.6 4.8 multiply_reduce_fusion.2
  512.3 16.3 %fusion.85 = (bf16[200,768]{1,0:T(8,128)(2,1)S(1)}, bf16[200,768]{1,0:T(8,128)(2,1)S(1)}) fusion(bf16[394,768]{1,0:T(8,128)(2,1)S(1)} %multiply_reduce_fusion.2, bf16[394,768]{1,0:T(8,128)(2,1)} %fusion.28), kind=kCustom, calls=%all-reduce-scatter.4 | all-reduce-scatter fusion | flops 614401 | bytes 1825280
  528.7 3.8 collective-permute-start.18
  532.5 7.2 %convolution_bitcast_fusion.1 = f32[1,768,1536]{2,1,0:T(8,128)} fusion(bf16[1024,768]{1,0:T(8,128)(2,1)} %bitcast.25, bf16[1024,1536]{1,0:T(8,128)(2,1)} %copy-done.18), kind=kOutput, calls=%fused_computation.17 | convolution fusion | flops 2415919104 | bytes 9437184 | tf_op jit(solution)/shard_map/dot_general | solution.py:222
  541.0 2.2 concatenate.21
  544.1 44.1 %all-reduce.21 = (f32[768,16]{0,1:T(8,128)S(1)}, f32[768]{0:T(1024)S(1)}, f32[768]{0:T(1024)S(1)}, f32[768]{0:T(1024)S(1)}, f32[768]{0:T(1024)S(1)}) all-reduce(f32[768,16]{0,1:T(8,128)S(1)} %fusion.92, f32[768]{0:T(1024)S(1)} %get-tuple-element.14, ...), channel_id=8, replica_groups=mesh['dp'=16,'tensor'=2] {'dp','tensor'}, use_global_device_ids=true, to_apply=%region_26.28.clone | all-reduce | flops 15360 | bytes 122880
  590.6 3.3 concatenate.19
  594.5 2.7 add_add_fusion.2
  597.2 4.4 reduce-scatter.12.cloned.1.call-done
  (244 shorter events, 61.9 us)
Async XLA Ops:
  7.2 236.4 %copy-start = (bf16[1,1536,768]{2,1,0:T(8,128)(2,1)S(1)}, bf16[1,1536,768]{2,1,0:T(8,128)(2,1)}, u32[]{:S(2)}) copy-start(bf16[1,1536,768]{2,1,0:T(8,128)(2,1)} %param.25) | copy-start | bytes 7077892
  7.2 60.9 %copy-start.27 = (bf16[48,384]{1,0:T(8,128)(2,1)S(1)}, bf16[48,384]{1,0:T(8,128)(2,1)}, u32[]{:S(2)}) copy-start(bf16[48,384]{1,0:T(8,128)(2,1)} %param.18) | copy-start | bytes 110596
  7.2 81.2 %all-gather.6.cloned.1.call-start = ((), (), s32[]{:S(2)}) async-start(), calls=%async_computation.6 | async-start | bytes 1880064 | tf_op jit(solution)/shard_map/all_gather | solution.py:46
  50.5 41.5 %copy-start.22 = (s32[394,2]{1,0:T(8,128)}, s32[394,2]{1,0:T(8,128)S(1)}, u32[]{:S(2)}) copy-start(s32[394,2]{1,0:T(8,128)S(1)} %copy.94) | copy-start | bytes 9460
  58.4 33.6 %copy-start.34 = (f32[197]{0:T(256)}, f32[197]{0:T(256)S(1)}, u32[]{:S(2)}) copy-start(f32[197]{0:T(256)S(1)} %fusion.47) | copy-start | bytes 2368
  58.4 33.6 %copy-start.30 = (f32[197]{0:T(256)}, f32[197]{0:T(256)S(1)}, u32[]{:S(2)}) copy-start(f32[197]{0:T(256)S(1)} %fusion.79) | copy-start | bytes 2368
  100.6 5.6 copy-start.13
  102.2 4.5 copy-start.11
  107.6 18.9 %copy-start.40 = (u32[32]{0:T(128)S(1)}, u32[32]{0:T(128)}, u32[]{:S(2)}) copy-start(u32[32]{0:T(128)} %constant.164) | copy-start | bytes 388
  107.6 20.2 %copy-start.39 = (bf16[768]{0:T(1024)(128)(2,1)S(1)}, bf16[768]{0:T(1024)(128)(2,1)}, u32[]{:S(2)}) copy-start(bf16[768]{0:T(1024)(128)(2,1)} %get-tuple-element.23) | copy-start | bytes 4612
  107.6 20.8 %copy-start.4 = (bf16[197,768]{1,0:T(8,128)(2,1)S(1)}, bf16[197,768]{1,0:T(8,128)(2,1)}, u32[]{:S(2)}) copy-start(bf16[197,768]{1,0:T(8,128)(2,1)} %param.16) | copy-start | bytes 907780
  108.3 19.6 %copy-start.16 = (bf16[394,384]{0,1:T(8,128)(2,1)}, bf16[394,384]{0,1:T(8,128)(2,1)S(1)}, u32[]{:S(2)}) copy-start(bf16[394,384]{0,1:T(8,128)(2,1)S(1)} %convert_element_type.124) | copy-start | bytes 907780
  124.1 3.8 collective-permute-start.15
  128.4 9.7 %copy-start.5 = (bf16[203,768]{1,0:T(8,128)(2,1)}, bf16[203,768]{1,0:T(8,128)(2,1)S(1)}, u32[]{:S(2)}) copy-start(bf16[203,768]{1,0:T(8,128)(2,1)S(1)} %concatenate.18) | copy-start | bytes 935428
  146.4 7.4 %copy-start.38 = (bf16[48,16]{0,1:T(8,128)(2,1)S(1)}, bf16[48,16]{0,1:T(8,128)(2,1)}, u32[]{:S(2)}) copy-start(bf16[48,16]{0,1:T(8,128)(2,1)} %param.19) | copy-start | bytes 4612
  146.4 42.8 %copy-start.23 = (s32[394,2]{1,0:T(8,128)S(1)}, s32[394,2]{1,0:T(8,128)}, u32[]{:S(2)}) copy-start(s32[394,2]{1,0:T(8,128)} %copy-done.22) | copy-start | bytes 9460
  149.3 52.8 %copy-start.19 = (bf16[197,768]{1,0:T(8,128)(2,1)S(1)}, bf16[197,768]{1,0:T(8,128)(2,1)}, u32[]{:S(2)}) copy-start(bf16[197,768]{1,0:T(8,128)(2,1)} %param.29) | copy-start | bytes 907780
  149.3 89.6 %all-to-all-start = ((bf16[16,64,768]{2,1,0:T(8,128)(2,1)}), bf16[16,64,768]{2,1,0:T(8,128)(2,1)}, u32[]{:S(2)}, u32[]{:S(2)}) async-start(bf16[16,64,768]{2,1,0:T(8,128)(2,1)} %broadcast_select_fusion.1), calls=%async_computation | async-start | bytes 3145728 | tf_op jit(solution)/shard_map/all_to_all | solution.py:67
  153.8 30.9 %collective-permute-start = (bf16[48,16]{0,1:T(8,128)(2,1)S(1)}, bf16[48,16]{0,1:T(8,128)(2,1)S(1)}, u32[]{:S(2)}, u32[]{:S(2)}) collective-permute-start(bf16[48,16]{0,1:T(8,128)(2,1)S(1)} %copy-done.38), channel_id=1, source_target_pairs={{0,2},{2,4},{4,6},{6,8},{8,10},{10,12},{12,14},{14,16},{16,18},{18... | collective-permute-start | bytes 4616 | tf_op jit(solution)/shard_map/ppermute | solution.py:24
  184.8 5.8 collective-permute-start.1
  184.8 5.8 collective-permute-start.8
  190.6 5.7 collective-permute-start.2
  190.6 5.8 collective-permute-start.9
  196.3 5.7 collective-permute-start.3
  196.4 13.3 %collective-permute-start.10 = (bf16[48,16]{0,1:T(8,128)(2,1)S(1)}, bf16[48,16]{0,1:T(8,128)(2,1)S(1)}, u32[]{:S(2)}, u32[]{:S(2)}) collective-permute-start(bf16[48,16]{0,1:T(8,128)(2,1)S(1)} %collective-permute-done.9), channel_id=1, source_target_pairs={{2,0},{4,2},{6,4},{8,6},{10,8},{12,10},{14,12},{16,14},{18,16},{20... | collective-permute-start | bytes 4616 | tf_op jit(solution)/shard_map/ppermute | solution.py:26
  202.1 10.9 %collective-permute-start.4 = (bf16[48,16]{0,1:T(8,128)(2,1)S(1)}, bf16[48,16]{0,1:T(8,128)(2,1)S(1)}, u32[]{:S(2)}, u32[]{:S(2)}) collective-permute-start(bf16[48,16]{0,1:T(8,128)(2,1)S(1)} %collective-permute-done.3), channel_id=1, source_target_pairs={{0,2},{2,4},{4,6},{6,8},{8,10},{10,12},{12,14},{14,16},{16,18},{18... | collective-permute-start | bytes 4616 | tf_op jit(solution)/shard_map/ppermute | solution.py:24
  209.7 4.6 collective-permute-start.11
  213.0 5.7 collective-permute-start.5
  214.3 5.7 collective-permute-start.12
  218.7 5.7 collective-permute-start.6
  220.1 14.3 %collective-permute-start.13 = (bf16[48,16]{0,1:T(8,128)(2,1)S(1)}, bf16[48,16]{0,1:T(8,128)(2,1)S(1)}, u32[]{:S(2)}, u32[]{:S(2)}) collective-permute-start(bf16[48,16]{0,1:T(8,128)(2,1)S(1)} %collective-permute-done.12), channel_id=1, source_target_pairs={{2,0},{4,2},{6,4},{8,6},{10,8},{12,10},{14,12},{16,14},{18,16},{20... | collective-permute-start | bytes 4616 | tf_op jit(solution)/shard_map/ppermute | solution.py:26
  224.5 14.4 %collective-permute-start.7 = (bf16[48,16]{0,1:T(8,128)(2,1)S(1)}, bf16[48,16]{0,1:T(8,128)(2,1)S(1)}, u32[]{:S(2)}, u32[]{:S(2)}) collective-permute-start(bf16[48,16]{0,1:T(8,128)(2,1)S(1)} %collective-permute-done.6), channel_id=1, source_target_pairs={{0,2},{2,4},{4,6},{6,8},{8,10},{10,12},{12,14},{14,16},{16,18},{18... | collective-permute-start | bytes 4616 | tf_op jit(solution)/shard_map/ppermute | solution.py:24
  234.4 18.7 %collective-permute-start.14 = (bf16[48,16]{0,1:T(8,128)(2,1)S(1)}, bf16[48,16]{0,1:T(8,128)(2,1)S(1)}, u32[]{:S(2)}, u32[]{:S(2)}) collective-permute-start(bf16[48,16]{0,1:T(8,128)(2,1)S(1)} %collective-permute-done.13), channel_id=1, source_target_pairs={{2,0},{4,2},{6,4},{8,6},{10,8},{12,10},{14,12},{16,14},{18,16},{20... | collective-permute-start | bytes 4616 | tf_op jit(solution)/shard_map/ppermute | solution.py:26
  243.6 4.8 copy-start.43
  248.4 5.4 copy-start.7
  248.4 5.7 copy-start.28
  248.4 36.5 %all-to-all-start.1 = ((bf16[16,64,768]{2,1,0:T(8,128)(2,1)}), bf16[16,64,768]{2,1,0:T(8,128)(2,1)}, u32[]{:S(2)}, u32[]{:S(2)}) async-start(bf16[16,64,768]{2,1,0:T(8,128)(2,1)} %bitcast.156), calls=%async_computation.1 | async-start | bytes 3145728 | tf_op jit(solution)/shard_map/all_to_all | solution.py:82
  365.1 8.3 %copy-start.24 = (bf16[16,64,768]{2,1,0:T(8,128)(2,1)}, bf16[16,64,768]{2,1,0:T(8,128)(2,1)S(1)}, u32[]{:S(2)}) copy-start(bf16[16,64,768]{2,1,0:T(8,128)(2,1)S(1)} %all_to_all.20) | copy-start | bytes 4718596
  365.1 8.3 %copy-start.41 = (bf16[1,768,1536]{2,1,0:T(8,128)(2,1)S(1)}, bf16[1,768,1536]{2,1,0:T(8,128)(2,1)}, u32[]{:S(2)}) copy-start(bf16[1,768,1536]{2,1,0:T(8,128)(2,1)} %param.24) | copy-start | bytes 7077892
  373.3 3.7 copy-start.18
  377.1 37.0 %all-to-all-start.3 = ((bf16[16,64,768]{2,1,0:T(8,128)(2,1)}), bf16[16,64,768]{2,1,0:T(8,128)(2,1)S(1)}, u32[]{:S(2)}, u32[]{:S(2)}) async-start(bf16[16,64,768]{2,1,0:T(8,128)(2,1)} %bitcast.157), calls=%async_computation.3 | async-start | bytes 3145728 | tf_op jit(solution)/shard_map/all_to_all | solution.py:82
  382.1 215.1 %reduce-scatter.14.cloned.1.call-start = ((), (), s32[]{:S(2)}) async-start(), calls=%async_computation.8 | async-start | bytes 1253376 | tf_op jit(solution)/shard_map/reduce_scatter | solution.py:262
  433.7 18.0 %copy-start.6 = (bf16[203,768]{1,0:T(8,128)(2,1)S(1)}, bf16[203,768]{1,0:T(8,128)(2,1)}, u32[]{:S(2)}) copy-start(bf16[203,768]{1,0:T(8,128)(2,1)} %copy-done.5) | copy-start | bytes 935428
  434.4 19.0 %copy-start.20 = (bf16[197,768]{1,0:T(8,128)(2,1)S(1)}, bf16[197,768]{1,0:T(8,128)(2,1)}, u32[]{:S(2)}) copy-start(bf16[197,768]{1,0:T(8,128)(2,1)} %param.29) | copy-start | bytes 907780
  447.3 3.9 collective-permute-start.17
  453.3 14.7 %copy-start.10 = (f32[197,768]{1,0:T(8,128)}, f32[197,768]{1,0:T(8,128)S(1)}, u32[]{:S(2)}) copy-start(f32[197,768]{1,0:T(8,128)S(1)} %get-tuple-element.32) | copy-start | bytes 1815556
  453.3 12.0 %copy-start.17 = (bf16[394,384]{0,1:T(8,128)(2,1)S(1)}, bf16[394,384]{0,1:T(8,128)(2,1)}, u32[]{:S(2)}) copy-start(bf16[394,384]{0,1:T(8,128)(2,1)} %copy-done.16) | copy-start | bytes 907780
  453.3 14.7 %copy-start.36 = (f32[197]{0:T(256)}, f32[197]{0:T(256)S(1)}, u32[]{:S(2)}) copy-start(f32[197]{0:T(256)S(1)} %negate_multiply_fusion.1) | copy-start | bytes 2368
  465.3 3.8 copy-start.12
  468.1 133.5 %reduce-scatter.12.cloned.1.call-start = ((), (), s32[]{:S(2)}) async-start(), calls=%async_computation.7 | async-start | bytes 3760128 | tf_op jit(solution)/shard_map/reduce_scatter | solution.py:261
  469.0 4.0 copy-start.3
  477.7 6.0 copy-start.14
  484.2 3.9 copy-start.21
  505.6 4.9 copy-start.42
  528.6 11.1 %copy-start.26 = (bf16[200,768]{1,0:T(8,128)(2,1)}, bf16[200,768]{1,0:T(8,128)(2,1)S(1)}, u32[]{:S(2)}) copy-start(bf16[200,768]{1,0:T(8,128)(2,1)S(1)} %get-tuple-element.30) | copy-start | bytes 921604
  528.6 11.0 %copy-start.25 = (bf16[200,768]{1,0:T(8,128)(2,1)}, bf16[200,768]{1,0:T(8,128)(2,1)S(1)}, u32[]{:S(2)}) copy-start(bf16[200,768]{1,0:T(8,128)(2,1)S(1)} %get-tuple-element.29) | copy-start | bytes 921604
  528.7 14.9 %copy-start.35 = (f32[197]{0:T(256)S(1)}, f32[197]{0:T(256)}, u32[]{:S(2)}) copy-start(f32[197]{0:T(256)} %copy-done.34) | copy-start | bytes 2368
  528.7 14.9 %copy-start.31 = (f32[197]{0:T(256)S(1)}, f32[197]{0:T(256)}, u32[]{:S(2)}) copy-start(f32[197]{0:T(256)} %copy-done.30) | copy-start | bytes 2368
  528.7 15.4 %copy-start.32 = (f32[768]{0:T(1024)S(1)}, f32[768]{0:T(1024)}, u32[]{:S(2)}) copy-start(f32[768]{0:T(1024)} %get-tuple-element.12) | copy-start | bytes 9220
  528.7 15.4 %copy-start.33 = (f32[768]{0:T(1024)S(1)}, f32[768]{0:T(1024)}, u32[]{:S(2)}) copy-start(f32[768]{0:T(1024)} %get-tuple-element.16) | copy-start | bytes 9220
  528.7 12.3 %collective-permute-start.18 = (bf16[3,768]{1,0:T(4,128)(2,1)S(1)}, bf16[3,768]{1,0:T(4,128)(2,1)S(1)}, u32[]{:S(2)}, u32[]{:S(2)}) collective-permute-start(bf16[3,768]{1,0:T(4,128)(2,1)S(1)} %slice.39), channel_id=1, source_target_pairs={{0,1},{2,3},{4,5},{6,7},{8,9},{10,11},{12,13},{14,15},{16,17},{18,... | collective-permute-start | bytes 13832
  539.7 54.8 %copy-start.37 = (f32[197]{0:T(256)S(1)}, f32[197]{0:T(256)}, u32[]{:S(2)}) copy-start(f32[197]{0:T(256)} %copy-done.36) | copy-start | bytes 2368
  539.7 50.9 %collective-permute-start.16 = (bf16[3,768]{1,0:T(4,128)(2,1)S(1)}, bf16[3,768]{1,0:T(4,128)(2,1)S(1)}, u32[]{:S(2)}, u32[]{:S(2)}) collective-permute-start(bf16[3,768]{1,0:T(4,128)(2,1)S(1)} %slice.37), channel_id=1, source_target_pairs={{0,1},{2,3},{4,5},{6,7},{8,9},{10,11},{12,13},{14,15},{16,17},{18,... | collective-permute-start | bytes 13832
  541.0 60.6 %copy-start.1 = (bf16[1,1536,768]{2,1,0:T(8,128)(2,1)S(1)}, bf16[1,1536,768]{2,1,0:T(8,128)(2,1)}, u32[]{:S(2)}) copy-start(bf16[1,1536,768]{2,1,0:T(8,128)(2,1)} %param.25) | copy-start | bytes 7077892
  (5 other events, 9.6 us)
Sparse Core Ops, SparseCore 0:
  10.4 43.3 all-gather.5
  468.2 61.6 reduce-scatter.13
  534.3 67.1 reduce-scatter.11
